TPU v7x, 32 devices: a whole 2x2x4 slice. The times are simulated.
32 devices in a mesh: graph: 16 (over z, y, x), rep: 2 (over core).
Axes of the slice: x: 2, y: 2, z: 4, core: 2. Of those that a mesh axis runs over, the one named last changes fastest.
Arguments:
- grad_out: bfloat16 [8192, 256], P(('graph', 'rep')), may hold values from -6 to 6
- pre_act: bfloat16 [8192, 256], P(('graph', 'rep')), may hold values from -6 to 6
- aggregated: bfloat16 [8192, 256], P(('graph', 'rep')), may hold values from -0.3125 to 0.3125
- weight: bfloat16 [256, 256], replicated, may hold values from -0.375 to 0.375
- adj_tiles: bfloat16 [16, 2, 16, 2, 128, 128], P('graph', 'rep'), may hold values from 0 to 0.039794922
- tile_row: int32 [16, 2, 16, 2], P('graph', 'rep'), may hold values from 0 to 1
- tile_col: int32 [16, 2, 16, 2], P('graph', 'rep'), may hold values from 0 to 3
- tile_count: int32 [16, 2, 16], P('graph', 'rep'), may hold values from 0 to 2, as said below
- node_perm: int32 [16, 512], P('graph'), may hold values from 0 to 511, each once within a row
Outputs:
- input_grad: bfloat16 [8192, 256], P(('graph', 'rep'))
- weight_grad: float32 [256, 256], replicated
- relu_grad: bfloat16 [8192, 256], P(('graph', 'rep'))
Inputs may be any that keep to these rules, and one draw needn't show every extreme that they name: tile_count[g, r, g] is 2 for every partition g and replica r. `node_perm`: each row is a permutation.
All inputs are finite; a program needn't handle non-finite values.
Results may differ from a plain program's by a relative error of at most 0.0049.
Values may be sent and summed in bfloat16 or wider, within the bound.
A program may use at most 128 MiB of HBM per device.

v0:
```python
import jax
import jax.numpy as jnp
from jax import lax
from jax.sharding import PartitionSpec as P


def tile_products(running, sources, row_count, local_tiles, local_row, local_col, local_count):
    piece_parts = sources.shape[0] // row_count
    tile_size = local_tiles.shape[-1]
    feature_width = sources.shape[1]
    blocks = sources.reshape(piece_parts, row_count // tile_size, tile_size, feature_width)
    part_index = jnp.arange(piece_parts, dtype=jnp.int32)
    for slot_index in range(local_tiles.shape[1]):
        chosen = blocks[part_index, local_row[:, slot_index]]
        product = jnp.einsum(
            "kab,kac->kbc", local_tiles[:, slot_index], chosen, preferred_element_type=jnp.float32
        )
        alive = (local_count > slot_index).astype(jnp.float32)
        running = running.at[local_col[:, slot_index]].add(product * alive[:, None, None])
    return running


def body(
    grad_out, pre_act, aggregated, weight, adj_tiles, tile_row, tile_col, tile_count, node_perm
):
    row_count = grad_out.shape[0]
    feature_width = weight.shape[0]
    relu_grad = jnp.where(pre_act > 0, grad_out, jnp.zeros_like(grad_out))
    partial_weight = lax.dot_general(
        aggregated, relu_grad, (((0,), (0,)), ((), ())), preferred_element_type=jnp.float32
    )
    local_tiles = adj_tiles[0, 0]
    local_row = tile_row[0, 0]
    local_col = tile_col[0, 0]
    local_count = tile_count[0, 0]
    local_perm = node_perm[0]
    tile_size = local_tiles.shape[-1]
    col_blocks = lax.axis_size("rep") * (row_count // tile_size)
    empty = jnp.zeros((col_blocks, tile_size, feature_width), jnp.float32)
    back_agg = lax.dot_general(
        relu_grad, weight, (((1,), (1,)), ((), ())), preferred_element_type=jnp.float32
    ).astype(jnp.bfloat16)
    running = tile_products(
        empty,
        lax.all_gather(back_agg, "graph", axis=0, tiled=True),
        row_count,
        local_tiles,
        local_row,
        local_col,
        local_count,
    )
    partial_grad = running.reshape(col_blocks * tile_size, feature_width)
    input_grad = lax.psum_scatter(
        jnp.take(partial_grad, local_perm, axis=0), "rep", scatter_dimension=0, tiled=True
    ).astype(jnp.bfloat16)
    weight_grad = lax.psum(partial_weight, ("graph", "rep"))
    return (input_grad, weight_grad, relu_grad)


def solution(mesh):
    placed = (
        P(("graph", "rep"), None),
        P(("graph", "rep"), None),
        P(("graph", "rep"), None),
        P(),
        P("graph", "rep", None, None, None, None),
        P("graph", "rep", None, None),
        P("graph", "rep", None, None),
        P("graph", "rep", None),
        P("graph", None),
    )
    return jax.shard_map(
        body,
        mesh=mesh,
        in_specs=placed,
        out_specs=(P(("graph", "rep"), None), P(), P(("graph", "rep"), None)),
        check_vma=False,
    )
```

profile of v0, /device:TPU:0, one launch (start us, length us, event | category | flops | bytes accessed | tf_op | source)
XLA Modules:
  0.0 160.9 jit_solution(16786216906860122379)
XLA Ops:
  8.0 0.0 copy-start
  8.0 0.0 copy-start.2
  8.0 0.0 all-gather.2.cloned.1.call-start
  8.1 1.1 compare_select_fusion
  9.1 0.0 copy-done
  9.2 0.0 copy-start.1
  9.2 0.9 convolution_convert_fusion
  10.0 0.0 all-gather.2.cloned.1.call-update
  10.1 0.0 all-reduce.2.cloned.1.call-start
  10.1 1.8 %convolution_bitcast_fusion = f32[256,256]{0,1:T(8,128)} fusion(bf16[256,256]{1,0:T(8,128)(2,1)S(1)} %compare_select_fusion, bf16[256,256]{1,0:T(8,128)(2,1)} %param.11), kind=kOutput, calls=%fused_computation.7 | convolution fusion | flops 33554432 | bytes 524288 | tf_op jit(solution)/shard_map/dot_general | solution.py:29
  12.0 0.0 all-reduce.2.cloned.1.call-update
  12.0 0.0 reduce-scatter.2.cloned.1.call-start
  12.0 0.7 compare_select_fusion.1
  12.7 0.7 compare_and_fusion
  13.4 0.8 fusion.10
  14.2 0.8 fusion.6
  14.9 0.7 fusion.1
  15.6 0.0 copy-done.2
  15.6 0.1 copy.25
  15.7 60.0 %all-gather.2.cloned.1.call-done = bf16[4096,256]{1,0:T(8,128)(2,1)} async-done(((bf16[256,256]{1,0:T(8,128)(2,1)}), bf16[4096,256]{1,0:T(8,128)(2,1)}) %all-gather.2.cloned.1.call-update) | async-done | bytes 2097168 | tf_op jit(solution)/shard_map/all_gather | solution.py:45
  75.7 3.2 %gather_fusion.1 = bf16[16,128,256]{2,1,0:T(8,128)(2,1)} fusion(bf16[16,2,128,256]{3,2,1,0:T(8,128)(2,1)} %bitcast.44, s32[16]{0:T(128)S(1)} %get-tuple-element.9), kind=kCustom, calls=%fused_computation.1 | custom fusion | bytes 2097280 | tf_op jit(solution)/shard_map/gather | solution.py:14
  78.9 0.0 copy-done.1
  78.9 2.2 %gather_fusion = bf16[16,128,256]{2,1,0:T(8,128)(2,1)S(1)} fusion(bf16[16,2,128,256]{3,2,1,0:T(8,128)(2,1)} %bitcast.45, s32[16]{0:T(128)S(1)} %get-tuple-element.10), kind=kCustom, calls=%fused_computation | custom fusion | bytes 2097280 | tf_op jit(solution)/shard_map/gather | solution.py:14
  81.1 1.8 %multiply_bitcast_fusion.1 = f32[16,128,256]{1,2,0:T(8,128)} fusion(bf16[16,128,256]{2,1,0:T(8,128)(2,1)S(1)} %gather_fusion, f32[16]{0:T(128)S(1)} %get-tuple-element.14, bf16[16,2,128,128]{3,2,0,1:T(8,128)(2,1)S(1)} %bitcast.42), kind=kOutput, calls=%fused_computation.6 | convolution fusion | flops 134742016 | bytes 3670528 | tf_op jit(solution)/shard_map/kab,kac->kbc/dot_general | solution.py:15
  83.0 1.9 %copy.18 = f32[16,128,256]{2,1,0:T(8,128)S(1)} copy(f32[16,128,256]{1,2,0:T(8,128)} %multiply_bitcast_fusion.1) | data formatting | bytes 4194304 | tf_op jit(solution)/shard_map/mul | solution.py:19
  84.9 3.1 %multiply_bitcast_fusion = f32[16,128,256]{1,2,0:T(8,128)} fusion(bf16[16,128,256]{2,1,0:T(8,128)(2,1)} %gather_fusion.1, f32[16]{0:T(128)S(1)} %get-tuple-element.13, bf16[16,2,128,128]{3,2,0,1:T(8,128)(2,1)S(1)} %bitcast.43), kind=kOutput, calls=%fused_computation.5 | convolution fusion | flops 134742016 | bytes 3670528 | tf_op jit(solution)/shard_map/kab,kac->kbc/dot_general | solution.py:15
  88.0 2.9 %copy.20 = f32[16,128,256]{2,1,0:T(8,128)} copy(f32[16,128,256]{1,2,0:T(8,128)} %multiply_bitcast_fusion) | data formatting | bytes 4194304 | tf_op jit(solution)/shard_map/mul | solution.py:19
  90.9 2.2 %scatter_fusion = f32[4,128,256]{2,1,0:T(8,128)S(1)} fusion(f32[4,128,256]{2,1,0:T(8,128)S(1)} %broadcast_in_dim.10, s32[16]{0:T(128)S(1)} %get-tuple-element.12, f32[16,128,256]{2,1,0:T(8,128)S(1)} %copy.18), kind=kCustom, calls=%fused_computation.3 | custom fusion | flops 524288 | bytes 6291520 | tf_op jit(solution)/shard_map/scatter-add | solution.py:19
  93.1 3.5 %scatter_fusion.1 = f32[4,128,256]{2,1,0:T(8,128)S(1)} fusion(f32[4,128,256]{2,1,0:T(8,128)S(1)} %scatter_fusion, s32[16]{0:T(128)S(1)} %get-tuple-element.11, f32[16,128,256]{2,1,0:T(8,128)} %copy.20), kind=kCustom, calls=%fused_computation.4 | custom fusion | flops 524288 | bytes 6291520 | tf_op jit(solution)/shard_map/scatter-add | solution.py:19
  96.6 1.6 gather_fusion.2
  98.2 0.9 broadcast_select_fusion
  99.1 0.0 reduce-scatter.2.cloned.1.call-update
  99.1 51.0 %all-reduce.2.cloned.1.call-done = f32[256,256]{0,1:T(8,128)} async-done(((f32[256,256]{0,1:T(8,128)}), f32[256,256]{0,1:T(8,128)}) %all-reduce.2.cloned.1.call-update) | async-done | bytes 262160 | tf_op jit(solution)/shard_map/psum | solution.py:56
  150.1 1.8 %copy.21 = f32[256,256]{1,0:T(8,128)} copy(f32[256,256]{0,1:T(8,128)} %all-reduce.2.cloned.1.call-done) | data formatting | bytes 524288
  151.9 0.0 reduce-scatter.2.cloned.1.call-done
  151.9 1.6 %convert_element_type.31 = bf16[256,256]{1,0:T(8,128)(2,1)} convert(f32[256,256]{1,0:T(8,128)} %reduce-scatter.2.cloned.1.call-done) | non-fusion elementwise | flops 65536 | bytes 393216 | tf_op jit(solution)/shard_map/convert_element_type | solution.py:55
  (2 shorter events, 0.0 us)
Async XLA Ops:
  8.0 1.1 copy-start
  8.0 7.6 %copy-start.2 = (bf16[1,1,16,2,128,128]{5,4,3,2,1,0:T(8,128)(2,1)S(1)}, bf16[1,1,16,2,128,128]{5,4,3,2,1,0:T(8,128)(2,1)}, u32[]{:S(2)}) copy-start(bf16[1,1,16,2,128,128]{5,4,3,2,1,0:T(8,128)(2,1)} %param.13) | copy-start | bytes 3145732
  8.0 67.7 %all-gather.2.cloned.1.call-start = ((), (), s32[]{:S(2)}) async-start(), calls=%async_computation.1 | async-start | bytes 2228224 | tf_op jit(solution)/shard_map/all_gather | solution.py:45
  9.2 69.8 %copy-start.1 = (bf16[256,256]{1,0:T(8,128)(2,1)}, bf16[256,256]{1,0:T(8,128)(2,1)S(1)}, u32[]{:S(2)}) copy-start(bf16[256,256]{1,0:T(8,128)(2,1)S(1)} %compare_select_fusion) | copy-start | bytes 393220
  10.1 140.0 %all-reduce.2.cloned.1.call-start = ((), (), s32[]{:S(2)}) async-start(), calls=%async_computation.3 | async-start | bytes 524288 | tf_op jit(solution)/shard_map/psum | solution.py:56
  12.0 139.9 %reduce-scatter.2.cloned.1.call-start = ((), (), s32[]{:S(2)}) async-start(), calls=%async_computation.2 | async-start | bytes 786432 | tf_op jit(solution)/shard_map/reduce_scatter | solution.py:53
Sparse Core Ops, SparseCore 0:
  12.2 63.4 all-gather.1
  99.3 6.6 reduce-scatter.1
Sparse Core Ops, SparseCore 1:
  17.5 132.5 all-reduce.1
where the time goes:
time: 161 us
  waiting for transfers between devices  111 us (69%)
  between operations  15.6 us (10%)
  local copies, waits for them, and re-layouts  13.7 us (9%)
  other arithmetic  12.8 us (8%)
  matrix products  7.62 us (5%)
    all_gather x1, waiting for transfers between devices, body(): lax.all_gather(back_agg, 'graph', axis=0, tiled=True)  60 us
    psum x1, waiting for transfers between devices, body(): weight_grad = lax.psum(partial_weight, ('graph', 'rep'))  51 us
    scatter-add x2, other arithmetic, tile_products(): running.at[local_col[:, slot_index]].add(product * alive[:, None, None])  5.67 us
    gather x2, local copies, waits for them, and re-layouts, tile_products(): chosen = blocks[part_index, local_row[:, slot_index]]  5.41 us
    dot_general x2, matrix products, tile_products(): jnp.einsum('kab,kac->kbc', local_tiles[:, slot_index], chosen, preferred_...  4.91 us
    mul x2, local copies, waits for them, and re-layouts, tile_products(): product * alive[:, None, None]  4.82 us
  transfers between devices with their start and end apart: 3, of which 2 were waited for; matrix products, arithmetic and copies ran while one was open for 19% of the time, Pallas kernels for 0%

commit v1 on v0

--- a/solution.py
+++ b/solution.py
@@ -1,7 +1,27 @@
+import functools
 import jax
 import jax.numpy as jnp
 from jax import lax
 from jax.sharding import PartitionSpec as P
+
+
+def part_the_tokens(incoming_x, axis_id, pos_dim):
+    long_array = lax.axis_size(axis_id)
+    tmp = lax.axis_index(axis_id)
+    inter, next_value = (long_array, tmp)
+    right_arr, local_part = (incoming_x, 1)
+    while local_part < inter:
+        far_arr = lax.ppermute(
+            right_arr, axis_id, tuple(((ii, ii ^ local_part) for ii in range(inter)))
+        )
+        high = jnp.concatenate([right_arr, far_arr], axis=pos_dim)
+        moved = jnp.concatenate([far_arr, right_arr], axis=pos_dim)
+        right_arr = jnp.where(next_value & local_part == 0, high, moved)
+        local_part = 2 * local_part
+    return right_arr
+
+
+arrange_cubes = functools.partial(part_the_tokens, axis_id="graph", pos_dim=0)
 
 
 def tile_products(running, sources, row_count, local_tiles, local_row, local_col, local_count):
@@ -41,13 +61,7 @@
         relu_grad, weight, (((1,), (1,)), ((), ())), preferred_element_type=jnp.float32
     ).astype(jnp.bfloat16)
     running = tile_products(
-        empty,
-        lax.all_gather(back_agg, "graph", axis=0, tiled=True),
-        row_count,
-        local_tiles,
-        local_row,
-        local_col,
-        local_count,
+        empty, arrange_cubes(back_agg), row_count, local_tiles, local_row, local_col, local_count
     )
     partial_grad = running.reshape(col_blocks * tile_size, feature_width)
     input_grad = lax.psum_scatter(

time: 161 us -> 183 us (1.14)
  waiting for transfers between devices: 111 us -> 126 us
  starting transfers between devices: 0.12 us -> 8.94 us
    ppermute x0 -> x4, waiting for transfers between devices: none -> 62.5 us  [part_the_tokens(): lax.ppermute(right_arr, axis_id, tuple(((ii, ii ^ local_part) for ii in r...]
    all_gather x1 -> x0, waiting for transfers between devices: 60 us -> none  [body(): lax.all_gather(back_agg, 'graph', axis=0, tiled=True)]
    psum x1, waiting for transfers between devices: 51 us -> 63.4 us  [body(): weight_grad = lax.psum(partial_weight, ('graph', 'rep'))]
    ppermute x0 -> x4, starting transfers between devices: none -> 8.86 us  [part_the_tokens(): lax.ppermute(right_arr, axis_id, tuple(((ii, ii ^ local_part) for ii in r...]
    select_n x0 -> x4, other arithmetic: none -> 2.63 us  [part_the_tokens(): right_arr = jnp.where(next_value & local_part == 0, high, moved)]
    gather x2, local copies, waits for them, and re-layouts: 5.41 us -> 3.21 us  [tile_products(): chosen = blocks[part_index, local_row[:, slot_index]]]
  transfers between devices with their start and end apart: 3 -> 6, of which waited for: 2 -> 5; matrix products, arithmetic and copies ran while one was open for 19% -> 16% of each run, Pallas kernels for 0% -> 0%
where the time goes in v1:
time: 183 us; the launch traced here: 182 us
  waiting for transfers between devices  126 us (69%)
  between operations  15.7 us (9%)
  local copies, waits for them, and re-layouts  12.5 us (7%)
  other arithmetic  11.9 us (7%)
  starting transfers between devices  8.94 us (5%)
  matrix products  7.28 us (4%)
    psum x1, waiting for transfers between devices, body(): weight_grad = lax.psum(partial_weight, ('graph', 'rep'))  63.4 us
    ppermute x4, waiting for transfers between devices, part_the_tokens(): lax.ppermute(right_arr, axis_id, tuple(((ii, ii ^ local_part) for ii in r...  62.5 us
    ppermute x4, starting transfers between devices, part_the_tokens(): lax.ppermute(right_arr, axis_id, tuple(((ii, ii ^ local_part) for ii in r...  8.86 us
    dot_general x2, matrix products, tile_products(): jnp.einsum('kab,kac->kbc', local_tiles[:, slot_index], chosen, preferred_...  6.14 us
    scatter-add x2, other arithmetic, tile_products(): running.at[local_col[:, slot_index]].add(product * alive[:, None, None])  5.67 us
    mul x2, local copies, waits for them, and re-layouts, tile_products(): product * alive[:, None, None]  4.82 us
  transfers between devices with their start and end apart: 6, of which 5 were waited for; matrix products, arithmetic and copies ran while one was open for 16% of the time, Pallas kernels for 0%

profile of v1, /device:TPU:0, one launch (start us, length us, event | category | flops | bytes accessed | tf_op | source)
XLA Modules:
  0.0 182.2 jit_solution(8298315513594558520)
XLA Ops:
  8.0 0.0 copy-start
  8.0 0.0 copy-start.4
  8.0 0.0 all-reduce.2.cloned.1.call-start
  8.1 1.0 compare_select_fusion
  9.1 0.0 copy-done
  9.1 0.0 copy-start.2
  9.1 0.2 convolution_convert_fusion
  9.4 3.0 %collective-permute-start = (bf16[256,256]{1,0:T(8,128)(2,1)S(1)}, bf16[256,256]{1,0:T(8,128)(2,1)S(1)}, u32[]{:S(2)}, u32[]{:S(2)}) collective-permute-start(bf16[256,256]{1,0:T(8,128)(2,1)S(1)} %convolution_convert_fusion), channel_id=1, source_target_pairs={{0,2},{2,0},{4,6},{6,4},{8,10},{10,8},{12,14},{14,12},{16,18},{18,... | collective-permute-start | bytes 393224 | tf_op jit(solution)/shard_map/ppermute | solution.py:14
  12.4 3.5 %collective-permute-done = bf16[256,256]{1,0:T(8,128)(2,1)S(1)} collective-permute-done((bf16[256,256]{1,0:T(8,128)(2,1)S(1)}, bf16[256,256]{1,0:T(8,128)(2,1)S(1)}, u32[]{:S(2)}, u32[]{:S(2)}) %collective-permute-start) | collective-permute-done | bytes 131104 | tf_op jit(solution)/shard_map/ppermute | solution.py:14
  15.9 0.1 maximum_select_fusion.3
  16.0 0.0 copy-start.5
  16.0 0.0 copy-start.3
  16.0 1.8 %collective-permute-start.1 = (bf16[512,256]{1,0:T(8,128)(2,1)S(1)}, bf16[512,256]{1,0:T(8,128)(2,1)S(1)}, u32[]{:S(2)}, u32[]{:S(2)}) collective-permute-start(bf16[512,256]{1,0:T(8,128)(2,1)S(1)} %maximum_select_fusion.3), channel_id=1, source_target_pairs={{0,4},{2,6},{4,0},{6,2},{8,12},{10,14},{12,8},{14,10},{16,20},{18,... | collective-permute-start | bytes 786440 | tf_op jit(solution)/shard_map/ppermute | solution.py:14
  17.8 5.7 %collective-permute-done.1 = bf16[512,256]{1,0:T(8,128)(2,1)S(1)} collective-permute-done((bf16[512,256]{1,0:T(8,128)(2,1)S(1)}, bf16[512,256]{1,0:T(8,128)(2,1)S(1)}, u32[]{:S(2)}, u32[]{:S(2)}) %collective-permute-start.1) | collective-permute-done | bytes 262176 | tf_op jit(solution)/shard_map/ppermute | solution.py:14
  23.6 0.2 maximum_select_fusion.2
  23.8 1.6 collective-permute-start.2
  25.4 0.0 copy-done.4
  25.4 0.9 convolution_bitcast_fusion
  26.3 0.0 all-reduce.2.cloned.1.call-update
  26.3 0.0 reduce-scatter.2.cloned.1.call-start
  26.4 0.0 copy-start.8
  26.4 0.0 copy-start.6
  26.4 0.0 copy-start.7
  26.4 9.8 %collective-permute-done.2 = bf16[1024,256]{1,0:T(8,128)(2,1)S(1)} collective-permute-done((bf16[1024,256]{1,0:T(8,128)(2,1)S(1)}, bf16[1024,256]{1,0:T(8,128)(2,1)S(1)}, u32[]{:S(2)}, u32[]{:S(2)}) %collective-permute-start.2) | collective-permute-done | bytes 524320 | tf_op jit(solution)/shard_map/ppermute | solution.py:14
  36.2 0.2 maximum_select_fusion.1
  36.5 0.0 copy-done.2
  36.5 2.5 %collective-permute-start.3 = (bf16[2048,256]{1,0:T(8,128)(2,1)S(1)}, bf16[2048,256]{1,0:T(8,128)(2,1)}, u32[]{:S(2)}, u32[]{:S(2)}) collective-permute-start(bf16[2048,256]{1,0:T(8,128)(2,1)S(1)} %maximum_select_fusion.1), channel_id=1, source_target_pairs={{0,16},{2,18},{4,20},{6,22},{8,24},{10,26},{12,28},{14,30},{16,0},... | collective-permute-start | bytes 3145736 | tf_op jit(solution)/shard_map/ppermute | solution.py:14
  38.9 0.0 copy-done.5
  38.9 0.0 copy-done.3
  38.9 1.0 copy.25
  40.0 0.0 copy-done.8
  40.0 0.0 copy-done.6
  40.0 0.0 copy-done.7
  40.1 43.4 %collective-permute-done.3 = bf16[2048,256]{1,0:T(8,128)(2,1)} collective-permute-done((bf16[2048,256]{1,0:T(8,128)(2,1)S(1)}, bf16[2048,256]{1,0:T(8,128)(2,1)}, u32[]{:S(2)}, u32[]{:S(2)}) %collective-permute-start.3) | collective-permute-done | bytes 1048608 | tf_op jit(solution)/shard_map/ppermute | solution.py:14
  83.5 2.1 %maximum_select_fusion = bf16[4096,256]{1,0:T(8,128)(2,1)S(1)} fusion(bf16[2048,256]{1,0:T(8,128)(2,1)} %collective-permute-done.3, bf16[2048,256]{1,0:T(8,128)(2,1)S(1)} %maximum_select_fusion.1, pred[]{:T(512)S(6)} %eq.12), kind=kLoop, calls=%fused_computation.5 | loop fusion | flops 9437184 | bytes 4194305 | tf_op jit(solution)/shard_map/jit(_where)/select_n | solution.py:19
  85.6 0.0 copy-start.1
  85.6 1.6 gather_fusion.1
  87.2 1.6 gather_fusion
  88.8 0.0 copy-done.1
  88.8 3.1 %multiply_bitcast_fusion = f32[16,128,256]{1,2,0:T(8,128)} fusion(bf16[16,128,256]{2,1,0:T(8,128)(2,1)} %gather_fusion.1, f32[16]{0:T(128)S(1)} %get-tuple-element.13, bf16[16,2,128,128]{3,2,0,1:T(8,128)(2,1)S(1)} %bitcast.44), kind=kOutput, calls=%fused_computation.6 | convolution fusion | flops 134742016 | bytes 3670528 | tf_op jit(solution)/shard_map/kab,kac->kbc/dot_general | solution.py:35
  91.9 1.9 %copy.20 = f32[16,128,256]{2,1,0:T(8,128)S(1)} copy(f32[16,128,256]{1,2,0:T(8,128)} %multiply_bitcast_fusion) | data formatting | bytes 4194304 | tf_op jit(solution)/shard_map/mul | solution.py:39
  93.8 3.1 %multiply_bitcast_fusion.1 = f32[16,128,256]{1,2,0:T(8,128)} fusion(bf16[16,128,256]{2,1,0:T(8,128)(2,1)} %gather_fusion, f32[16]{0:T(128)S(1)} %get-tuple-element.14, bf16[16,2,128,128]{3,2,0,1:T(8,128)(2,1)S(1)} %bitcast.45), kind=kOutput, calls=%fused_computation.7 | convolution fusion | flops 134742016 | bytes 3670528 | tf_op jit(solution)/shard_map/kab,kac->kbc/dot_general | solution.py:35
  96.9 2.9 %copy.18 = f32[16,128,256]{2,1,0:T(8,128)} copy(f32[16,128,256]{1,2,0:T(8,128)} %multiply_bitcast_fusion.1) | data formatting | bytes 4194304 | tf_op jit(solution)/shard_map/mul | solution.py:39
  99.8 3.5 %scatter_fusion = f32[4,128,256]{2,1,0:T(8,128)S(1)} fusion(f32[4,128,256]{2,1,0:T(8,128)S(1)} %broadcast_in_dim.10, s32[16]{0:T(128)S(1)} %get-tuple-element.12, f32[16,128,256]{2,1,0:T(8,128)} %copy.18), kind=kCustom, calls=%fused_computation.3 | custom fusion | flops 524288 | bytes 6291520 | tf_op jit(solution)/shard_map/scatter-add | solution.py:39
  103.3 2.2 %scatter_fusion.1 = f32[4,128,256]{2,1,0:T(8,128)S(1)} fusion(f32[4,128,256]{2,1,0:T(8,128)S(1)} %scatter_fusion, s32[16]{0:T(128)S(1)} %get-tuple-element.11, f32[16,128,256]{2,1,0:T(8,128)S(1)} %copy.20), kind=kCustom, calls=%fused_computation.4 | custom fusion | flops 524288 | bytes 6291520 | tf_op jit(solution)/shard_map/scatter-add | solution.py:39
  105.5 1.6 gather_fusion.2
  107.1 0.9 broadcast_select_fusion
  108.0 0.0 reduce-scatter.2.cloned.1.call-update
  108.0 63.4 %all-reduce.2.cloned.1.call-done = f32[256,256]{0,1:T(8,128)} async-done(((f32[256,256]{0,1:T(8,128)}), f32[256,256]{0,1:T(8,128)}) %all-reduce.2.cloned.1.call-update) | async-done | bytes 262160 | tf_op jit(solution)/shard_map/psum | solution.py:70
  171.4 1.8 copy.21
  173.2 0.0 reduce-scatter.2.cloned.1.call-done
  173.2 1.6 convert_element_type.31
  (7 shorter events, 0.1 us)
Async XLA Ops:
  8.0 1.1 copy-start
  8.0 17.3 %copy-start.4 = (bf16[256,256]{1,0:T(8,128)(2,1)S(1)}, bf16[256,256]{1,0:T(8,128)(2,1)}, u32[]{:S(2)}) copy-start(bf16[256,256]{1,0:T(8,128)(2,1)} %param.11) | copy-start | bytes 393220
  8.0 163.4 %all-reduce.2.cloned.1.call-start = ((), (), s32[]{:S(2)}) async-start(), calls=%async_computation.2 | async-start | bytes 524288 | tf_op jit(solution)/shard_map/psum | solution.py:70
  9.1 27.3 %copy-start.2 = (bf16[256,256]{1,0:T(8,128)(2,1)}, bf16[256,256]{1,0:T(8,128)(2,1)S(1)}, u32[]{:S(2)}) copy-start(bf16[256,256]{1,0:T(8,128)(2,1)S(1)} %compare_select_fusion) | copy-start | bytes 393220
  9.4 6.5 %collective-permute-start = (bf16[256,256]{1,0:T(8,128)(2,1)S(1)}, bf16[256,256]{1,0:T(8,128)(2,1)S(1)}, u32[]{:S(2)}, u32[]{:S(2)}) collective-permute-start(bf16[256,256]{1,0:T(8,128)(2,1)S(1)} %convolution_convert_fusion), channel_id=1, source_target_pairs={{0,2},{2,0},{4,6},{6,4},{8,10},{10,8},{12,14},{14,12},{16,18},{18,... | collective-permute-start | bytes 393224 | tf_op jit(solution)/shard_map/ppermute | solution.py:14
  16.0 23.0 %copy-start.5 = (s32[1,512]{1,0:T(1,128)S(1)}, s32[1,512]{1,0:T(1,128)}, u32[]{:S(2)}) copy-start(s32[1,512]{1,0:T(1,128)} %param.17) | copy-start | bytes 6148
  16.0 23.0 %copy-start.3 = (bf16[1,1,16,2,128,128]{5,4,3,2,1,0:T(8,128)(2,1)S(1)}, bf16[1,1,16,2,128,128]{5,4,3,2,1,0:T(8,128)(2,1)}, u32[]{:S(2)}) copy-start(bf16[1,1,16,2,128,128]{5,4,3,2,1,0:T(8,128)(2,1)} %param.13) | copy-start | bytes 3145732
  16.0 7.6 %collective-permute-start.1 = (bf16[512,256]{1,0:T(8,128)(2,1)S(1)}, bf16[512,256]{1,0:T(8,128)(2,1)S(1)}, u32[]{:S(2)}, u32[]{:S(2)}) collective-permute-start(bf16[512,256]{1,0:T(8,128)(2,1)S(1)} %maximum_select_fusion.3), channel_id=1, source_target_pairs={{0,4},{2,6},{4,0},{6,2},{8,12},{10,14},{12,8},{14,10},{16,20},{18,... | collective-permute-start | bytes 786440 | tf_op jit(solution)/shard_map/ppermute | solution.py:14
  23.8 12.4 %collective-permute-start.2 = (bf16[1024,256]{1,0:T(8,128)(2,1)S(1)}, bf16[1024,256]{1,0:T(8,128)(2,1)S(1)}, u32[]{:S(2)}, u32[]{:S(2)}) collective-permute-start(bf16[1024,256]{1,0:T(8,128)(2,1)S(1)} %maximum_select_fusion.2), channel_id=1, source_target_pairs={{0,8},{2,10},{4,12},{6,14},{8,0},{10,2},{12,4},{14,6},{16,24},{18,... | collective-permute-start | bytes 1572872 | tf_op jit(solution)/shard_map/ppermute | solution.py:14
  26.3 146.9 %reduce-scatter.2.cloned.1.call-start = ((), (), s32[]{:S(2)}) async-start(), calls=%async_computation.1 | async-start | bytes 786432 | tf_op jit(solution)/shard_map/reduce_scatter | solution.py:67
  26.4 13.6 %copy-start.8 = (s32[1,1,16]{2,1,0:T(1,128)S(1)}, s32[1,1,16]{2,1,0:T(1,128)}, u32[]{:S(2)}) copy-start(s32[1,1,16]{2,1,0:T(1,128)} %param.16) | copy-start | bytes 196
  26.4 13.6 %copy-start.6 = (s32[1,1,16,2]{2,3,1,0:T(2,128)S(1)}, s32[1,1,16,2]{2,3,1,0:T(2,128)}, u32[]{:S(2)}) copy-start(s32[1,1,16,2]{2,3,1,0:T(2,128)} %param.14) | copy-start | bytes 388
  26.4 13.6 %copy-start.7 = (s32[1,1,16,2]{2,3,1,0:T(2,128)S(1)}, s32[1,1,16,2]{2,3,1,0:T(2,128)}, u32[]{:S(2)}) copy-start(s32[1,1,16,2]{2,3,1,0:T(2,128)} %param.15) | copy-start | bytes 388
  36.5 47.1 %collective-permute-start.3 = (bf16[2048,256]{1,0:T(8,128)(2,1)S(1)}, bf16[2048,256]{1,0:T(8,128)(2,1)}, u32[]{:S(2)}, u32[]{:S(2)}) collective-permute-start(bf16[2048,256]{1,0:T(8,128)(2,1)S(1)} %maximum_select_fusion.1), channel_id=1, source_target_pairs={{0,16},{2,18},{4,20},{6,22},{8,24},{10,26},{12,28},{14,30},{16,0},... | collective-permute-start | bytes 3145736 | tf_op jit(solution)/shard_map/ppermute | solution.py:14
  85.6 3.2 %copy-start.1 = (bf16[1,1,16,2,128,128]{5,4,2,3,1,0:T(8,128)(2,1)S(1)}, bf16[1,1,16,2,128,128]{5,4,2,3,1,0:T(8,128)(2,1)}, u32[]{:S(2)}) copy-start(bf16[1,1,16,2,128,128]{5,4,2,3,1,0:T(8,128)(2,1)} %copy.25) | copy-start | bytes 3145732
Sparse Core Ops, SparseCore 0:
  26.4 144.9 all-reduce.1
Sparse Core Ops, SparseCore 1:
  108.1 8.3 reduce-scatter.1
